TPU v7x, 256 devices: a whole 4x4x8 slice. The times are simulated.
256 devices in a mesh: dp: 4 (over y_hi, core), seq: 64 (over y_lo, x, z).
Axes of the slice: x: 4, y: 4 (y_hi: 2, y_lo: 2; y = y_hi * 2 + y_lo), z: 8, core: 2. Of those that a mesh axis runs over, the one named last changes fastest.
Arguments:
- inputs: bfloat16 [4096, 8, 1536], P('seq', 'dp'), may hold values from -6 to 6
- query_proj: bfloat16 [4096, 8, 1536], P('seq', 'dp'), may hold values from -8 to 8
- key_proj: bfloat16 [4096, 8, 1536], P('seq', 'dp'), may hold values from -8 to 8
- value_proj: bfloat16 [4096, 8, 1536], P('seq', 'dp'), may hold values from -6 to 6
- lengths: int32 [8], P('dp'), may hold values from 1024 to 4096, as said below
- out_weight: bfloat16 [1536, 1536], P('dp'), may hold values from -0.15625 to 0.15625
- norm_gain: float32 [1536], replicated, may hold values from 0.25 to 1.75
- conv_weight: float32 [31, 1536], replicated, may hold values from -1 to 1
- cotangent: bfloat16 [4096, 8, 1536], P('seq', 'dp'), may hold values from -6 to 6
Outputs:
- block_out: bfloat16 [4096, 8, 1536], P('seq', 'dp')
- grad_input: bfloat16 [4096, 8, 1536], P('seq', 'dp')
- grad_query: bfloat16 [4096, 8, 1536], P('seq', 'dp')
- grad_key: bfloat16 [4096, 8, 1536], P('seq', 'dp')
- grad_value: bfloat16 [4096, 8, 1536], P('seq', 'dp')
- grad_weight: float32 [1536, 1536], P('dp')
- grad_gain: float32 [1536], replicated
- grad_conv: float32 [31, 1536], replicated
Inputs may be any that keep to these rules, and one draw needn't show every extreme that they name: `lengths`: some utterance has all 4096 frames valid in every draw.
All inputs are finite; a program needn't handle non-finite values.
Results may differ from a plain program's by a relative error of at most 0.028.
Values may be sent and summed in bfloat16 or wider, within the bound.
No kernel may reach another device: no remote copies, remote signals or barrier semaphores. Data moves between devices by JAX's collectives and lax.ppermute only.
A program may use at most 128 MiB of HBM per device.

v0:
```python
import functools
import math

import jax
import jax.numpy as jnp
from jax import lax
from jax.experimental import pallas as pl
from jax.experimental.pallas import tpu as pltpu
from jax.sharding import Mesh
from jax.sharding import PartitionSpec as P

H = 16
DH = 96
EPSILON = 1e-05
SEQ = ("yl", "x", "z")
DP = ("yh", "c")
SWAP = [(0, 1), (1, 0)]
LOG2E = math.log2(math.e)
SCALE = 1.0 / math.sqrt(DH)
HALF = 32
RIM = 16
SLAB = 24
BQ = 512
BK = 1024
MASKED = -1e30
F32 = jnp.float32
BF16 = jnp.bfloat16
VMEM_LIMIT = 56 * 1024 * 1024


def lane_of(shape):
    return lax.broadcasted_iota(jnp.int32, shape, len(shape) - 1)


def roll(value, shift):
    return pltpu.roll(value, shift, 1)


def pack_rows(rows):
    lane = lane_of((SLAB, 128))
    rest = rows[SLAB:]
    filler = jnp.concatenate([roll(rest, 96), roll(rest, 64), roll(rest, 32)])
    return jnp.where(lane < DH, rows[:SLAB], filler)


def unpack_rows(slab):
    lane = lane_of((8, 128))
    rest = jnp.where(
        lane < 32,
        roll(slab[:8], 32),
        jnp.where(lane < 64, roll(slab[8:16], 64), roll(slab[16:], 96)),
    )
    rows = jnp.concatenate([slab, rest])
    return jnp.where(lane_of((HALF, 128)) < DH, rows, 0.0)


def pack_kernel(core_ref, *refs):
    sources, (mine_ref, theirs_ref) = refs[:-2], refs[-2:]
    core = core_ref[0]
    lane = lane_of((HALF, 128))
    for target, half in ((mine_ref, core), (theirs_ref, 1 - core)):
        start = pl.multiple_of(half * HALF, HALF)

        def step(index, carry, target=target, start=start):
            utterance, quad = index // 4, index % 4
            columns = pl.ds(pl.multiple_of(quad * 384, 128), 384)
            slabs = [[], [], [], []]
            for source in sources:
                wide = source[utterance, pl.ds(start, HALF), columns].astype(F32)
                t0, t1, t2 = wide[:, :128], wide[:, 128:256], wide[:, 256:]
                heads = (
                    t0,
                    roll(jnp.where(lane < 64, t1, t0), 32),
                    roll(jnp.where(lane < 32, t2, t1), 64),
                    roll(t2, 96),
                )
                for slab, rows in zip(slabs, heads):
                    slab.append(pack_rows(rows))
            for head, slab in enumerate(slabs):
                target[index * 4 + head] = jnp.concatenate(slab).astype(BF16)
            return carry

        lax.fori_loop(0, 8, step, 0)


def pack(core, *sources):
    shape = jax.ShapeDtypeStruct((2 * H, len(sources) * SLAB, 128), BF16)
    return pl.pallas_call(
        pack_kernel,
        out_shape=(shape, shape),
        in_specs=[pl.BlockSpec(memory_space=pltpu.SMEM)]
        + [pl.BlockSpec(memory_space=pltpu.VMEM)] * len(sources),
        out_specs=[pl.BlockSpec(memory_space=pltpu.VMEM)] * 2,
        compiler_params=pltpu.CompilerParams(vmem_limit_bytes=VMEM_LIMIT),
        cost_estimate=pl.CostEstimate(
            flops=0, bytes_accessed=len(sources) * 8 * 1024 * 1024, transcendentals=0
        ),
        name="pack",
    )(core, *sources)


def unpack_kernel(core_ref, mine_ref, theirs_ref, *targets):
    core = core_ref[0]
    lane = lane_of((HALF, 128))
    for source, half in ((mine_ref, core), (theirs_ref, 1 - core)):
        start = pl.multiple_of(half * HALF, HALF)

        def step(index, carry, source=source, start=start):
            utterance, quad = index // 4, index % 4
            slabs = [source[index * 4 + head].astype(F32) for head in range(4)]
            for at, target in enumerate(targets):
                a, b, c, d = [unpack_rows(slab[at * SLAB : (at + 1) * SLAB]) for slab in slabs]
                b, c, d = roll(b, 96), roll(c, 64), roll(d, 32)
                wide = [
                    jnp.where(lane < 96, a, b),
                    jnp.where(lane < 64, b, c),
                    jnp.where(lane < 32, c, d),
                ]
                columns = pl.ds(pl.multiple_of(quad * 384, 128), 384)
                wide = jnp.concatenate(wide, axis=1).astype(BF16)
                target[utterance, pl.ds(start, HALF), columns] = wide
            return carry

        lax.fori_loop(0, 8, step, 0)


def unpack(core, mine, theirs):
    count = mine.shape[1] // SLAB
    shape = jax.ShapeDtypeStruct((2, 2 * HALF, H * DH), BF16)
    return pl.pallas_call(
        unpack_kernel,
        out_shape=(shape,) * count,
        in_specs=[pl.BlockSpec(memory_space=pltpu.SMEM)]
        + [pl.BlockSpec(memory_space=pltpu.VMEM)] * 2,
        out_specs=[pl.BlockSpec(memory_space=pltpu.VMEM)] * count,
        compiler_params=pltpu.CompilerParams(vmem_limit_bytes=VMEM_LIMIT),
        cost_estimate=pl.CostEstimate(
            flops=0, bytes_accessed=count * 8 * 1024 * 1024, transcendentals=0
        ),
        name="unpack",
    )(core, mine, theirs)


def three_parts(value):
    high = value.astype(BF16).astype(F32)
    middle = (value - high).astype(BF16).astype(F32)
    return high, middle, value - high - middle


def place_parts(base, value):
    lane = lane_of(base.shape)
    high, middle, low = three_parts(value)
    base = jnp.where(lane == DH, high, base)
    base = jnp.where(lane == DH + 1, middle, base)
    return jnp.where(lane == DH + 2, low, base)


def across(lhs, rhs):
    return lax.dot_general(lhs, rhs, (((1,), (1,)), ((), ())), preferred_element_type=F32)


def forward_kernel(
    info_ref,
    own_ref,
    other_ref,
    mixed_ref,
    output_ref,
    plain_ref,
    query_ref,
    key_ref,
    value_ref,
    scores_a,
    scores_b,
):
    sources = own_ref.shape[0]
    valid, core = info_ref[0], info_ref[1]
    own_keys = sources * HALF
    keys = 2 * own_keys
    lane = lane_of((HALF, 128))
    row = lax.broadcasted_iota(jnp.int32, (HALF, 128), 0)

    def place_keys(source, slab_k, slab_v, half, begin):
        key = unpack_rows(slab_k)
        value = unpack_rows(slab_v)
        frame = source * (2 * HALF) + half * HALF + row
        bias = jnp.where(frame < valid, 0.0, MASKED)
        low = jnp.where(lane < DH, key, jnp.where(lane < DH + 3, 1.0, 0.0))
        low = jnp.where(lane == DH + 3, bias, low)
        at = pl.ds(pl.multiple_of(begin + source * HALF, HALF), HALF)
        key_ref[at, :128] = low.astype(BF16)
        key_ref[at, 128:] = key.astype(BF16)
        value_ref[at, :] = jnp.where(
            lane < DH, value, jnp.where(lane < DH + 3, 1.0, 0.0)
        ).astype(BF16)

    def place(source, carry):
        own = own_ref[source].astype(F32)
        other = other_ref[source].astype(F32)
        query = unpack_rows(own[:SLAB])
        scaled = query * (SCALE * LOG2E)
        high = scaled.astype(BF16).astype(F32)
        at = pl.ds(pl.multiple_of(source * HALF, HALF), HALF)
        plain_ref[at, :] = query.astype(BF16)
        query_ref[at, :128] = jnp.where(lane == DH + 3, 1.0, high).astype(BF16)
        query_ref[at, 128:] = (scaled - high).astype(BF16)
        place_keys(source, own[SLAB : 2 * SLAB], own[2 * SLAB :], core, 0)
        place_keys(source, other[SLAB : 2 * SLAB], other[2 * SLAB :], 1 - core, own_keys)
        return carry

    lax.fori_loop(0, sources, place, 0, unroll=2)

    blocks = own_keys // BQ

    def score_chunk(query, scores, chunk):
        part = across(query, key_ref[chunk * BK : (chunk + 1) * BK, :])
        scores[:, chunk * BK : (chunk + 1) * BK] = part
        best = part[:, :128]
        for tile in range(1, BK // 128):
            best = jnp.maximum(best, part[:, tile * 128 : (tile + 1) * 128])
        return best

    def rows_of(block):
        return pl.ds(pl.multiple_of(block * BQ, BQ), BQ)

    def first_scores():
        query = query_ref[rows_of(0), :]
        best = score_chunk(query, scores_a, 0)
        for chunk in range(1, keys // BK):
            best = jnp.maximum(best, score_chunk(query, scores_a, chunk))
        return jnp.max(best, axis=1, keepdims=True)

    def step(block, highest, scores, later):
        if later is not None:
            follow = query_ref[rows_of(block + 1), :]
        best = None
        total = None
        for chunk in range(keys // BK):
            if later is not None:
                more = score_chunk(follow, later, chunk)
                best = more if best is None else jnp.maximum(best, more)
            span = slice(chunk * BK, (chunk + 1) * BK)
            powers = jnp.exp2(scores[:, span] - highest).astype(BF16)
            mixed = jnp.dot(powers, value_ref[span, :], preferred_element_type=F32)
            total = mixed if total is None else total + mixed
        sums = total[:, DH : DH + 1]
        mixed = jnp.where(lane_of(total.shape) < DH, total / sums, 0.0)
        output_ref[rows_of(block), :] = mixed
        logs = highest + jnp.log2(sums)
        low = query_ref[rows_of(block), :128].astype(F32)
        query_ref[rows_of(block), :128] = place_parts(low, -logs).astype(BF16)
        for part in range(BQ // HALF):
            slab = pack_rows(mixed[part * HALF : (part + 1) * HALF])
            mixed_ref[block * (BQ // HALF) + part] = slab.astype(BF16)
        return None if later is None else jnp.max(best, axis=1, keepdims=True)

    def two_steps(pair, highest):
        highest = step(2 * pair, highest, scores_a, scores_b)
        return step(2 * pair + 1, highest, scores_b, scores_a)

    highest = lax.fori_loop(0, blocks // 2 - 1, two_steps, first_scores())
    highest = step(blocks - 2, highest, scores_a, scores_b)
    step(blocks - 1, highest, scores_b, None)


def attend(info, own, other):
    sources = own.shape[0]
    rows = sources * HALF
    return pl.pallas_call(
        forward_kernel,
        out_shape=(
            jax.ShapeDtypeStruct((sources, SLAB, 128), BF16),
            jax.ShapeDtypeStruct((rows, 128), F32),
            jax.ShapeDtypeStruct((rows, 128), BF16),
            jax.ShapeDtypeStruct((rows, 256), BF16),
            jax.ShapeDtypeStruct((2 * rows, 256), BF16),
            jax.ShapeDtypeStruct((2 * rows, 128), BF16),
        ),
        in_specs=[pl.BlockSpec(memory_space=pltpu.SMEM)]
        + [pl.BlockSpec(memory_space=pltpu.VMEM)] * 2,
        out_specs=[pl.BlockSpec(memory_space=pltpu.VMEM)] * 6,
        scratch_shapes=[pltpu.VMEM((BQ, 2 * rows), F32)] * 2,
        compiler_params=pltpu.CompilerParams(vmem_limit_bytes=VMEM_LIMIT),
        cost_estimate=pl.CostEstimate(
            flops=4 * rows * 2 * rows * 256,
            bytes_accessed=8 * 1024 * 1024,
            transcendentals=2 * rows * rows,
        ),
        name="attend",
    )(info, own, other)


def backward_kernel(
    grad_ref,
    output_ref,
    plain_ref,
    query_ref,
    key_ref,
    value_ref,
    grad_query_ref,
    own_ref,
    other_ref,
    key_total,
    value_total,
):
    own_keys = plain_ref.shape[0]
    keys = 2 * own_keys
    blocks = own_keys // BQ
    parts = BQ // HALF

    def step(block, carry):
        at = pl.ds(pl.multiple_of(block * BQ, BQ), BQ)
        grad = jnp.concatenate(
            [unpack_rows(grad_ref[block * parts + part].astype(F32)) for part in range(parts)]
        )
        centre = jnp.sum(grad * output_ref[at, :], axis=1, keepdims=True)
        grad_low = place_parts(grad, -centre).astype(BF16)
        grad_turned = grad.T[:DH].astype(BF16)
        query_turned = plain_ref[at, :].astype(F32).T[:DH].astype(BF16)
        query = query_ref[at, :]
        total = None
        for chunk in range(keys // BK):
            span = slice(chunk * BK, (chunk + 1) * BK)
            probs = jnp.exp2(across(query, key_ref[span, :]))
            grad_probs = across(grad_low, value_ref[span, :])
            grad_scores = (probs * grad_probs).astype(BF16)
            value_part = jnp.dot(grad_turned, probs.astype(BF16), preferred_element_type=F32)
            key_part = jnp.dot(query_turned, grad_scores, preferred_element_type=F32)
            value_total[:, span] += value_part
            key_total[:, span] += key_part
            more = jnp.dot(grad_scores, key_ref[span, :128], preferred_element_type=F32)
            total = more if total is None else total + more
        total = total * SCALE
        for part in range(parts):
            slab = pack_rows(total[part * HALF : (part + 1) * HALF])
            grad_query_ref[block * parts + part] = slab.astype(BF16)
        return carry

    key_total[...] = jnp.zeros_like(key_total)
    value_total[...] = jnp.zeros_like(value_total)
    lax.fori_loop(0, blocks, step, 0)

    for begin, target in ((0, own_ref), (own_keys, other_ref)):

        def turn(group, carry, begin=begin, target=target):
            at = pl.ds(pl.multiple_of(begin + group * 128, 128), 128)
            zeros = jnp.zeros((128 - DH, 128), F32)
            key = jnp.concatenate([key_total[:, at] * SCALE, zeros]).T
            value = jnp.concatenate([value_total[:, at], zeros]).T
            for part in range(128 // HALF):
                rows = slice(part * HALF, (part + 1) * HALF)
                slab = jnp.concatenate([pack_rows(key[rows]), pack_rows(value[rows])])
                target[group * (128 // HALF) + part] = slab.astype(target.dtype)
            return carry

        lax.fori_loop(0, own_keys // 128, turn, 0)


def attend_back(grad, output, plain, query, key, value):
    sources = grad.shape[0]
    rows = sources * HALF
    return pl.pallas_call(
        backward_kernel,
        out_shape=(
            jax.ShapeDtypeStruct((sources, SLAB, 128), BF16),
            jax.ShapeDtypeStruct((sources, 2 * SLAB, 128), F32),
            jax.ShapeDtypeStruct((sources, 2 * SLAB, 128), BF16),
        ),
        in_specs=[pl.BlockSpec(memory_space=pltpu.VMEM)] * 6,
        out_specs=[pl.BlockSpec(memory_space=pltpu.VMEM)] * 3,
        scratch_shapes=[pltpu.VMEM((DH, 2 * rows), F32)] * 2,
        compiler_params=pltpu.CompilerParams(vmem_limit_bytes=VMEM_LIMIT),
        cost_estimate=pl.CostEstimate(
            flops=10 * rows * 2 * rows * 256,
            bytes_accessed=8 * 1024 * 1024,
            transcendentals=2 * rows * rows,
        ),
        name="attend_back",
    )(grad, output, plain, query, key, value)


def with_halo(shard, width):
    count, length = (lax.axis_size(SEQ), shard.shape[1])
    up = [(i, i + 1) for i in range(count - 1)]
    down = [(j, i) for i, j in up]
    before = lax.ppermute(shard[:, length - width :], SEQ, up)
    after = lax.ppermute(shard[:, :width], SEQ, down)
    return jnp.concatenate([before, shard, after], axis=1)


def split_halves(total):
    high = total.astype(BF16)
    return high, (total - high.astype(F32)).astype(BF16)


def in_order(core, mine, theirs):
    first = jnp.where(core == 0, mine, theirs)
    second = jnp.where(core == 0, theirs, mine)
    return jnp.concatenate([first, second])


def to_pairs(core, *sources):
    mine, theirs = pack(core[None], *sources)
    theirs = lax.ppermute(theirs, "c", SWAP)
    return lax.all_to_all(in_order(core, mine, theirs), SEQ, 0, 0, tiled=True)


def exchange(blocks):
    return lax.all_to_all(blocks, SEQ, 0, 0, tiled=True)


def to_frames(core, blocks):
    got = blocks.reshape((2, -1) + blocks.shape[1:])
    mine = lax.dynamic_index_in_dim(got, core, keepdims=False)
    theirs = lax.dynamic_index_in_dim(got, 1 - core, keepdims=False)
    return unpack(core[None], mine, lax.ppermute(theirs, "c", SWAP))


def sum_parameters(flat_attn, flat_grad, small):
    core = lax.axis_index("c")
    width = flat_attn.shape[1]
    block = width // 4
    by_core = flat_attn.reshape(-1, 2, 2, block)
    mine = lax.dynamic_index_in_dim(by_core, core, axis=2, keepdims=False)
    theirs = lax.dynamic_index_in_dim(by_core, 1 - core, axis=2, keepdims=False)
    other_attn = lax.ppermute(theirs.reshape(-1, 2 * block), "c", SWAP)
    other_grad = lax.ppermute(flat_grad, "c", SWAP)
    small = small + lax.ppermute(small, "c", SWAP)
    rows = jnp.concatenate([mine.reshape(-1, 2 * block), other_attn])
    grads = jnp.concatenate([flat_grad, other_grad])
    partial = lax.dot_general(
        rows, grads, (((0,), (0,)), ((), ())), preferred_element_type=F32
    ).astype(BF16)
    count = small.shape[0] // 8
    small_blocks = small.astype(BF16).reshape(8, count, width)
    sent = jnp.concatenate(
        [partial.reshape(16, block // 8, width), jnp.tile(small_blocks, (2, 1, 1))], axis=1
    )
    got = lax.all_to_all(sent, ("yh", "yl", "x"), 0, 0, tiled=True)
    total = jnp.sum(got.astype(F32), axis=0).astype(BF16)
    big = total[: block // 8].reshape(8, block // 64, width)
    tail = jnp.broadcast_to(total[block // 8 :][None], (8, count, width))
    got = lax.all_to_all(jnp.concatenate([big, tail], axis=1), "z", 0, 0, tiled=True)
    total = jnp.sum(got.astype(F32), axis=0)
    small = total[block // 64 :]
    rows = jnp.concatenate([total[: block // 64], jnp.zeros((2, width), F32)])
    return rows, small


def finish_parameters(rows, small, block, width):
    count = small.shape[0]
    rows = rows.reshape(8, -1, width)[:, : block // 64].reshape(-1, width).astype(BF16)
    piece = jnp.concatenate([rows, *split_halves(small)])
    got = lax.all_to_all(
        jnp.broadcast_to(piece[None], (8,) + piece.shape), ("yl", "x"), 0, 0, tiled=True
    ).astype(F32)
    grad_weight = got[:, : block // 8].reshape(block, width)
    small = (got[:, block // 8 : block // 8 + count] + got[:, block // 8 + count :]).reshape(-1, width)
    return grad_weight, small[:-1], small[-1]


def per_device(
    inputs, query_proj, key_proj, value_proj, lengths, out_weight, norm_gain, conv_weight, cotangent
):
    frames, utterances, width = inputs.shape
    row_count = frames * utterances
    kernel_taps = conv_weight.shape[0]
    rim_width = (kernel_taps - 1) // 2
    core = lax.axis_index("c")
    place = lax.axis_index(SEQ)
    position = place * frames + jnp.arange(frames)
    keep_mask = (position[None, :] < lengths[:, None]).astype(F32)[:, :, None]
    all_lengths = in_order(core, lengths, lax.ppermute(lengths, "c", SWAP))
    pair_length = lax.dynamic_index_in_dim(all_lengths, place // H, keepdims=False)
    info = jnp.stack([pair_length, core])
    weight = lax.all_gather(out_weight, DP, axis=0, tiled=True)

    def turned(tensor):
        return tensor.transpose(1, 0, 2)

    wide_cotangent = with_halo(turned(cotangent), RIM)
    own = to_pairs(core, turned(query_proj), turned(key_proj), turned(value_proj))
    other = lax.ppermute(own, "c", SWAP)
    mixed, output, plain, query, key, value = attend(info, own, other)
    (attention,) = to_frames(core, exchange(mixed))
    flat_attn = attention.reshape(row_count, width)
    projected = jnp.dot(flat_attn, weight, preferred_element_type=F32)
    summed = turned(inputs).astype(F32) + projected.reshape(utterances, frames, width)
    centred = summed - jnp.mean(summed, axis=-1, keepdims=True)
    inverse = lax.rsqrt(jnp.mean(centred * centred, axis=-1, keepdims=True) + EPSILON)
    normed = centred * inverse
    conv_in = (normed * norm_gain * keep_mask).astype(BF16)
    padded = with_halo(conv_in, 2 * RIM).astype(F32)
    wide = frames + 2 * RIM
    wide_position = place * frames - RIM + jnp.arange(wide)
    wide_keep = (wide_position[None, :] < lengths[:, None]).astype(F32)[:, :, None]
    conv_wide = jnp.zeros((utterances, wide, width), F32)
    for offset in range(kernel_taps):
        begin = RIM - rim_width + offset
        conv_wide = conv_wide + conv_weight[offset] * padded[:, begin : begin + wide]
    conv_sum = conv_wide[:, RIM : RIM + frames]
    block_out = (keep_mask * (summed + jax.nn.silu(conv_sum))).astype(BF16)
    grad_wide = wide_cotangent.astype(F32) * wide_keep
    grad_out = grad_wide[:, RIM : RIM + frames]
    sigmoid_gate = jax.nn.sigmoid(conv_wide)
    grad_padded = (grad_wide * sigmoid_gate * (1.0 + conv_wide * (1.0 - sigmoid_gate))).astype(BF16)
    grad_padded = grad_padded.astype(F32)
    grad_centre = grad_padded[:, RIM : RIM + frames]
    grad_conv_in = jnp.zeros((utterances, frames, width), F32)
    tap_sums = []
    for offset in range(kernel_taps):
        begin = RIM + rim_width - offset
        grad_conv_in = grad_conv_in + conv_weight[offset] * grad_padded[:, begin : begin + frames]
        begin = 2 * RIM - rim_width + offset
        tap_sums.append(jnp.sum(padded[:, begin : begin + frames] * grad_centre, axis=(0, 1)))
    grad_raw = grad_conv_in * keep_mask
    small = jnp.concatenate([jnp.stack(tap_sums), jnp.sum(grad_raw * normed, axis=(0, 1))[None]])
    grad_normed = grad_raw * norm_gain
    grad_summed = (
        grad_out
        + (
            grad_normed
            - jnp.mean(grad_normed, axis=-1, keepdims=True)
            - normed * jnp.mean(grad_normed * normed, axis=-1, keepdims=True)
        )
        * inverse
    )
    grad_input = grad_summed.astype(BF16)
    flat_grad = grad_input.reshape(row_count, width)
    grad_flat = lax.dot_general(
        flat_grad, weight, (((1,), (1,)), ((), ())), preferred_element_type=F32
    )
    grad_attention = grad_flat.astype(BF16).reshape(utterances, frames, width)
    head_grad = to_pairs(core, grad_attention)
    rows, small = sum_parameters(flat_attn, flat_grad, small)
    head_grad, block_out, grad_input = lax.optimization_barrier(
        (head_grad, turned(block_out), turned(grad_input))
    )
    grad_q, grad_own, grad_other = attend_back(head_grad, output, plain, query, key, value)
    grad_pairs = (grad_own + lax.ppermute(grad_other, "c", SWAP).astype(F32)).astype(BF16)
    grad_pairs, rows = lax.optimization_barrier(
        (jnp.concatenate([grad_q, grad_pairs], axis=1), rows)
    )
    blocks = exchange(grad_pairs)
    rows = lax.all_gather(rows, "z", axis=0, tiled=True)
    blocks, rows = lax.optimization_barrier((blocks, rows))
    grad_weight, grad_conv, grad_gain = finish_parameters(rows, small, width // 4, width)
    grad_query, grad_key, grad_value = to_frames(core, blocks)
    return (
        block_out,
        grad_input,
        turned(grad_query),
        turned(grad_key),
        turned(grad_value),
        grad_weight,
        grad_gain,
        grad_conv,
    )


def solution(mesh):
    mesh = Mesh(mesh.devices.reshape(2, 2, 2, 4, 8), ("yh", "c", "yl", "x", "z"))
    split = P(SEQ, DP, None)
    in_specs = (split, split, split, split, P(DP), P(DP, None), P(), P(), split)
    out_specs = (split, split, split, split, split, P(DP, None), P(), P())
    return jax.shard_map(
        per_device, mesh=mesh, in_specs=in_specs, out_specs=out_specs, check_vma=False
    )
```

profile of v0, /device:TPU:8, one launch (start us, length us, event | category | flops | bytes accessed | tf_op | source)
XLA Modules:
  0.0 333.6 jit_solution(4614427905705546532)
XLA Ops:
  7.2 0.7 all-gather.2.cloned.1.call-update
  8.3 1.0 copy_bitcast_fusion
  9.3 0.8 copy.46
  10.0 4.8 %pack.2 = (bf16[32,72,128]{2,1,0:T(8,128)(2,1)}, bf16[32,72,128]{2,1,0:T(8,128)(2,1)}) custom-call(s32[1]{0:T(128)} %bitcast.core_ref, bf16[2,64,1536]{2,1,0:T(8,128)(2,1)} %bitcast.64, bf16[2,64,1536]{2,1,0:T(8,128)(2,1)} %get-tuple-element.165.refs_1_, bf16[2,64,1536]{2,1,0:T(8,128)(2,1)} %get-tuple-element.164.refs_2_), custom_call_target="tpu_custom_call" | custom-call | bytes 25165824 | tf_op jit(solution)/shard_map/pack/pallas_call | solution.py:88
  14.8 2.2 collective-permute-done.3
  17.0 1.1 broadcast_select_fusion.1
  18.3 45.5 %all_to_all.35.own_ref = bf16[64,72,128]{2,1,0:T(8,128)(2,1)S(1)} all-to-all(bf16[64,72,128]{2,1,0:T(8,128)(2,1)S(1)} %pad_maximum_fusion.1), channel_id=1, replica_groups=mesh['yh'=2,'c'=2,'yl'=2,'x'=4,'z'=8] {'yl','x','z'}, dimensions={0} | all-to-all | bytes 2359296 | tf_op jit(solution)/shard_map/all_to_all | solution.py:404
  64.6 2.1 collective-permute-done.2
  67.4 1.2 pad_add_fusion.1.info_ref
  68.6 1.0 copy-done.59
  69.6 16.9 %attend.1 = (bf16[64,24,128]{2,1,0:T(8,128)(2,1)}, f32[2048,128]{1,0:T(8,128)}, bf16[2048,128]{1,0:T(8,128)(2,1)}, bf16[2048,256]{1,0:T(8,128)(2,1)}, bf16[4096,...) custom-call(s32[2]{0:T(128)} %pad_add_fusion.1.info_ref, bf16[64,72,128]{2,1,0:T(8,128)(2,1)} %copy-done.3, ...), custom_call_target="tpu_custom_call" | custom-call | flops 8589934592 | bytes 8388608 | tf_op jit(solution)/shard_map/attend/pallas_call | solution.py:268
  86.6 5.7 %all-to-all-start.1 = ((bf16[64,24,128]{2,1,0:T(8,128)(2,1)}), bf16[64,24,128]{2,1,0:T(8,128)(2,1)S(1)}, u32[]{:S(2)}, u32[]{:S(2)}) async-start(bf16[64,24,128]{2,1,0:T(8,128)(2,1)} %get-tuple-element.33), calls=%async_computation.1 | async-start | bytes 786432 | tf_op jit(solution)/shard_map/all_to_all | solution.py:408
  92.3 3.5 %collective-permute-start = (bf16[2,16,1536]{2,1,0:T(8,128)(2,1)S(1)}, bf16[2,16,1536]{2,1,0:T(8,128)(2,1)S(1)}, u32[]{:S(2)}, u32[]{:S(2)}) collective-permute-start(bf16[2,16,1536]{2,1,0:T(8,128)(2,1)S(1)} %get-tuple-element.158), channel_id=1, source_target_pairs={{0,1},{1,2},{2,3},{3,4},{4,5},{5,6},{6,7},{7,8},{8,9},{9,10},{10,1... | collective-permute-start | bytes 294920 | tf_op jit(solution)/shard_map/ppermute | solution.py:385
  95.9 7.1 %collective-permute-start.1 = (bf16[2,16,1536]{2,1,0:T(8,128)(2,1)S(1)}, bf16[2,16,1536]{2,1,0:T(8,128)(2,1)S(1)}, u32[]{:S(2)}, u32[]{:S(2)}) collective-permute-start(bf16[2,16,1536]{2,1,0:T(8,128)(2,1)S(1)} %get-tuple-element.159), channel_id=1, source_target_pairs={{1,0},{2,1},{3,2},{4,3},{5,4},{6,5},{7,6},{8,7},{9,8},{10,9},{11,1... | collective-permute-start | bytes 294920 | tf_op jit(solution)/shard_map/ppermute | solution.py:386
  103.0 0.8 slice_reduce_fusion.30
  103.8 0.9 slice_reduce_fusion.31
  104.7 4.5 %all-to-all-done.1 = bf16[64,24,128]{2,1,0:T(8,128)(2,1)S(1)} async-done(((bf16[64,24,128]{2,1,0:T(8,128)(2,1)}), bf16[64,24,128]{2,1,0:T(8,128)(2,1)S(1)}, u32[]{:S(2)}, u32[]{:S(2)}) %all-to-all-start.1) | async-done | bytes 393248 | tf_op jit(solution)/shard_map/all_to_all | solution.py:408
  109.3 0.7 dynamic-slice_bitcast_fusion.2
  110.1 1.4 collective-permute-done.5.theirs_ref
  112.1 4.2 %unpack.2 = bf16[2,64,1536]{2,1,0:T(8,128)(2,1)} custom-call(s32[1]{0:T(128)} %bitcast.core_ref, bf16[32,24,128]{2,1,0:T(8,128)(2,1)} %get-tuple-element.157.mine_ref, bf16[32,24,128]{2,1,0:T(8,128)(2,1)} %copy-done.16), custom_call_target="tpu_custom_call" | custom-call | bytes 8388608 | tf_op jit(solution)/shard_map/unpack/pallas_call | solution.py:130
  116.3 3.3 %fusion.111 = (f32[2,64]{1,0:T(2,128)S(1)}, f32[2,64,1536]{2,1,0:T(8,128)S(1)}) fusion(bf16[2,64,1536]{2,1,0:T(8,128)(2,1)} %unpack.2, bf16[1536,1536]{1,0:T(8,128)(2,1)} %all-gather.2.cloned.1.call-done, bf16[64,2,1536]{2,1,0:T(2,128)(2,1)S(1)} %copy-done.13), kind=kOutput, calls=%fused_computation.284 | convolution fusion | flops 604569472 | bytes 6291968 | tf_op jit(solution)/shard_map/dot_general | solution.py:486
  120.2 0.7 fusion.109
  120.9 2.8 collective-permute-start.6
  123.7 7.3 %collective-permute-start.7 = (bf16[2,32,1536]{2,1,0:T(8,128)(2,1)S(1)}, bf16[2,32,1536]{2,1,0:T(8,128)(2,1)S(1)}, u32[]{:S(2)}, u32[]{:S(2)}) collective-permute-start(bf16[2,32,1536]{2,1,0:T(8,128)(2,1)S(1)} %get-tuple-element.155), channel_id=1, source_target_pairs={{1,0},{2,1},{3,2},{4,3},{5,4},{6,5},{7,6},{8,7},{9,8},{10,9},{11,1... | collective-permute-start | bytes 589832 | tf_op jit(solution)/shard_map/ppermute | solution.py:386
  131.0 1.2 convert_multiply_fusion
  132.3 0.8 constant_dynamic-slice_fusion.1
  133.2 1.0 copy.39
  135.7 5.2 %fusion.101 = (f32[2,96,1536]{2,1,0:T(8,128)S(1)}, f32[2,96,1536]{2,1,0:T(8,128)S(1)}) fusion(f32[2,96]{1,0:T(2,128)S(1)} %copy-done.56, bf16[2,16,1536]{2,1,0:T(8,128)(2,1)S(1)} %collective-permute-done.1, bf16[2,64,1536]{2,1,0:T(8,128)(2,1)S(1)} %bitcast.60, bf16[2,16,1536]{2,1,0:T(8,128)(2,1)S(1)} %collective-permute-done, ...), kind=kLoop, calls=%fused_computation.211 | loop fusion | flops 23003136 | bytes 39709440 | tf_op jit(solution)/shard_map/convert_element_type | solution.py:506
  140.9 0.9 fusion.52
  141.8 1.3 fusion.43
  143.2 5.3 %multiply_reduce_fusion = (f32[1536]{0:T(1024)S(1)}, f32[2,64]{1,0:T(2,128)S(1)}, f32[2,64]{1,0:T(2,128)S(1)}, f32[2,64,1536]{2,1,0:T(8,128)S(1)}) fusion(f32[2,64,1536]{2,1,0:T(8,128)S(1)} %get-tuple-element.163, f32[2,64]{1,0:T(2,128)S(1)} %copy-done.54, f32[2,64]{1,0:T(2,128)S(1)} %copy-done.50, f32[1536]{0:T(1024)S(1)} %copy-done.18, ...), kind=kLoop, calls=%fused_computation.202 | loop fusion | flops 13760768 | bytes 26157568 | tf_op jit(solution)/shard_map/reduce_sum | solution.py:516
  149.0 2.4 convolution_convert_fusion.1
  151.3 4.0 %pack.3 = (bf16[32,24,128]{2,1,0:T(8,128)(2,1)}, bf16[32,24,128]{2,1,0:T(8,128)(2,1)}) custom-call(s32[1]{0:T(128)} %bitcast.core_ref, bf16[2,64,1536]{2,1,0:T(8,128)(2,1)} %bitcast.65), custom_call_target="tpu_custom_call" | custom-call | bytes 8388608 | tf_op jit(solution)/shard_map/pack/pallas_call | solution.py:88
  155.7 0.9 fusion.35
  158.1 0.8 pad_maximum_fusion.3
  158.9 8.9 %all-to-all-start.2 = ((bf16[64,24,128]{2,1,0:T(8,128)(2,1)}), bf16[64,24,128]{2,1,0:T(8,128)(2,1)S(1)}, u32[]{:S(2)}, u32[]{:S(2)}) async-start(bf16[64,24,128]{2,1,0:T(8,128)(2,1)} %pad_maximum_fusion.3), calls=%async_computation.2 | async-start | bytes 786432 | tf_op jit(solution)/shard_map/all_to_all | solution.py:404
  167.9 0.8 convolution_convert_fusion
  168.8 1.8 pad_maximum_fusion
  170.6 13.9 %all-to-all-done.2.grad_ref = bf16[64,24,128]{2,1,0:T(8,128)(2,1)S(1)} async-done(((bf16[64,24,128]{2,1,0:T(8,128)(2,1)}), bf16[64,24,128]{2,1,0:T(8,128)(2,1)S(1)}, u32[]{:S(2)}, u32[]{:S(2)}) %all-to-all-start.2) | async-done | bytes 393248 | tf_op jit(solution)/shard_map/all_to_all | solution.py:404
  184.5 0.7 copy-done.9
  185.3 6.1 %all-to-all-start.3 = ((bf16[16,52,1536]{2,1,0:T(8,128)(2,1)}), bf16[16,52,1536]{2,1,0:T(8,128)(2,1)S(1)}, u32[]{:S(2)}, u32[]{:S(2)}) async-start(bf16[16,52,1536]{2,1,0:T(8,128)(2,1)} %pad_maximum_fusion), calls=%async_computation.3 | async-start | bytes 5505024 | tf_op jit(solution)/shard_map/all_to_all | solution.py:438
  191.3 30.9 %attend_back.1 = (bf16[64,24,128]{2,1,0:T(8,128)(2,1)}, f32[64,48,128]{2,1,0:T(8,128)}, bf16[64,48,128]{2,1,0:T(8,128)(2,1)}) custom-call(bf16[64,24,128]{2,1,0:T(8,128)(2,1)} %copy-done.9, f32[2048,128]{1,0:T(8,128)} %get-tuple-element.39.output_ref, bf16[2048,128]{1,0:T(8,128)(2,1)} %get-tuple-element.40.plain_ref, ...), custom_call_target="tpu_custom_call" | custom-call | flops 21474836480 | bytes 8388608 | tf_op jit(solution)/shard_map/attend_back/pallas_call | solution.py:361
  222.3 5.3 %all-to-all-done.3 = bf16[16,52,1536]{2,1,0:T(8,128)(2,1)S(1)} async-done(((bf16[16,52,1536]{2,1,0:T(8,128)(2,1)}), bf16[16,52,1536]{2,1,0:T(8,128)(2,1)S(1)}, u32[]{:S(2)}, u32[]{:S(2)}) %all-to-all-start.3) | async-done | bytes 2555936 | tf_op jit(solution)/shard_map/all_to_all | solution.py:438
  227.6 1.1 reduce_sum.381
  228.7 0.9 slice.694
  229.6 0.9 slice.693
  230.6 0.9 pad_maximum_fusion.4
  231.5 4.2 %all-to-all-start.4 = ((bf16[8,10,1536]{2,1,0:T(8,128)(2,1)}), bf16[8,10,1536]{2,1,0:T(8,128)(2,1)S(1)}, u32[]{:S(2)}, u32[]{:S(2)}) async-start(bf16[8,10,1536]{2,1,0:T(8,128)(2,1)} %pad_maximum_fusion.4), calls=%async_computation.4 | async-start | bytes 786432 | tf_op jit(solution)/shard_map/all_to_all | solution.py:442
  235.7 1.3 add_convert_fusion
  237.1 1.1 pad_maximum_fusion.2
  238.2 10.6 %all-to-all-done.4 = bf16[8,10,1536]{2,1,0:T(8,128)(2,1)S(1)} async-done(((bf16[8,10,1536]{2,1,0:T(8,128)(2,1)}), bf16[8,10,1536]{2,1,0:T(8,128)(2,1)S(1)}, u32[]{:S(2)}, u32[]{:S(2)}) %all-to-all-start.4) | async-done | bytes 245792 | tf_op jit(solution)/shard_map/all_to_all | solution.py:442
  249.0 6.1 %all-to-all-start.5 = ((bf16[64,72,128]{2,1,0:T(8,128)(2,1)}), bf16[64,72,128]{2,1,0:T(8,128)(2,1)S(1)}, u32[]{:S(2)}, u32[]{:S(2)}) async-start(bf16[64,72,128]{2,1,0:T(8,128)(2,1)} %pad_maximum_fusion.2), calls=%async_computation.5 | async-start | bytes 2359296 | tf_op jit(solution)/shard_map/all_to_all | solution.py:408
  255.1 46.8 %all_gather.7 = bf16[64,1536]{1,0:T(8,128)(2,1)S(1)} all-gather(bf16[8,1536]{1,0:T(8,128)(2,1)S(1)} %slice_select_fusion), channel_id=1, replica_groups=mesh['yh'=2,'c'=2,'yl'=2,'x'=4,'z'=8] {'z'}, dimensions={0}, use_global_device_ids=true | all-gather | bytes 221184 | tf_op jit(solution)/shard_map/all_gather | solution.py:544
  302.1 1.2 broadcast_in_dim.11
  303.2 5.8 %all-to-all-start.6 = ((bf16[8,56,1536]{2,1,0:T(8,128)(2,1)}), bf16[8,56,1536]{2,1,0:T(8,128)(2,1)S(1)}, u32[]{:S(2)}, u32[]{:S(2)}) async-start(bf16[8,56,1536]{2,1,0:T(8,128)(2,1)} %broadcast_in_dim.11), calls=%async_computation.6 | async-start | bytes 2752512 | tf_op jit(solution)/shard_map/all_to_all | solution.py:453
  309.0 0.9 dynamic-slice_bitcast_fusion
  310.1 1.2 copy.34
  311.3 1.1 copy.35
  312.4 0.8 copy-done.5
  313.3 4.9 %unpack.3 = (bf16[2,64,1536]{2,1,0:T(8,128)(2,1)}, bf16[2,64,1536]{2,1,0:T(8,128)(2,1)}, bf16[2,64,1536]{2,1,0:T(8,128)(2,1)}) custom-call(s32[1]{0:T(128)} %bitcast.core_ref, bf16[32,72,128]{2,1,0:T(8,128)(2,1)} %get-tuple-element.145.mine_ref, bf16[32,72,128]{2,1,0:T(8,128)(2,1)} %copy-done.5), custom_call_target="tpu_custom_call" | custom-call | bytes 25165824 | tf_op jit(solution)/shard_map/unpack/pallas_call | solution.py:130
  318.2 2.2 copy.36
  320.4 2.1 copy.37
  322.5 1.2 copy.38
  324.8 1.7 slice.698
  (215 shorter events, 8.4 us)
Async XLA Ops:
  7.2 1.0 copy-start.11
  7.2 1.1 copy-start.12
  7.2 2.1 copy-start.7
  7.2 109.1 %all-gather.2.cloned.1.call-start = ((), (), s32[]{:S(2)}) async-start(), calls=%async_computation.7 | async-start | bytes 5898240 | tf_op jit(solution)/shard_map/all_gather | solution.py:475
  14.8 2.2 collective-permute-start.3
  18.3 45.5 %copy-start.57 = (s32[2]{0:T(128)S(1)}, s32[2]{0:T(128)}, u32[]{:S(2)}) copy-start(s32[2]{0:T(128)} %param.13) | copy-start | bytes 28
  18.3 46.2 %copy-start.8 = (bf16[64,2,1536]{2,1,0:T(2,128)(2,1)S(1)}, bf16[64,2,1536]{2,1,0:T(2,128)(2,1)}, u32[]{:S(2)}) copy-start(bf16[64,2,1536]{2,1,0:T(2,128)(2,1)} %param.17) | copy-start | bytes 1179652
  63.8 4.8 %copy-start.3 = (bf16[64,72,128]{2,1,0:T(8,128)(2,1)}, bf16[64,72,128]{2,1,0:T(8,128)(2,1)S(1)}, u32[]{:S(2)}) copy-start(bf16[64,72,128]{2,1,0:T(8,128)(2,1)S(1)} %all_to_all.35.own_ref) | copy-start | bytes 3538948
  63.8 4.8 %collective-permute-start.4 = (bf16[64,72,128]{2,1,0:T(8,128)(2,1)S(1)}, bf16[64,72,128]{2,1,0:T(8,128)(2,1)S(1)}, u32[]{:S(2)}, u32[]{:S(2)}) collective-permute-start(bf16[64,72,128]{2,1,0:T(8,128)(2,1)S(1)} %all_to_all.35.own_ref), channel_id=1, source_target_pairs={{0,64},{64,0},{1,65},{65,1},{2,66},{66,2},{3,67},{67,3},{4,68},{68... | collective-permute-start | bytes 3538952 | tf_op jit(solution)/shard_map/ppermute | solution.py:482
  63.8 2.8 collective-permute-start.2
  68.6 1.0 copy-start.59
  86.6 16.4 %copy-start.17 = (f32[31,1536]{1,0:T(8,128)S(1)}, f32[31,1536]{1,0:T(8,128)}, u32[]{:S(2)}) copy-start(f32[31,1536]{1,0:T(8,128)} %param.16) | copy-start | bytes 571396
  86.6 22.7 %all-to-all-start.1 = ((bf16[64,24,128]{2,1,0:T(8,128)(2,1)}), bf16[64,24,128]{2,1,0:T(8,128)(2,1)S(1)}, u32[]{:S(2)}, u32[]{:S(2)}) async-start(bf16[64,24,128]{2,1,0:T(8,128)(2,1)} %get-tuple-element.33), calls=%async_computation.1 | async-start | bytes 786432 | tf_op jit(solution)/shard_map/all_to_all | solution.py:408
  92.3 24.0 %copy-start.13 = (bf16[64,2,1536]{2,1,0:T(2,128)(2,1)S(1)}, bf16[64,2,1536]{2,1,0:T(2,128)(2,1)}, u32[]{:S(2)}) copy-start(bf16[64,2,1536]{2,1,0:T(2,128)(2,1)} %param.9) | copy-start | bytes 1179652
  92.3 38.7 %collective-permute-start = (bf16[2,16,1536]{2,1,0:T(8,128)(2,1)S(1)}, bf16[2,16,1536]{2,1,0:T(8,128)(2,1)S(1)}, u32[]{:S(2)}, u32[]{:S(2)}) collective-permute-start(bf16[2,16,1536]{2,1,0:T(8,128)(2,1)S(1)} %get-tuple-element.158), channel_id=1, source_target_pairs={{0,1},{1,2},{2,3},{3,4},{4,5},{5,6},{6,7},{7,8},{8,9},{9,10},{10,1... | collective-permute-start | bytes 294920 | tf_op jit(solution)/shard_map/ppermute | solution.py:385
  95.9 35.2 %collective-permute-start.1 = (bf16[2,16,1536]{2,1,0:T(8,128)(2,1)S(1)}, bf16[2,16,1536]{2,1,0:T(8,128)(2,1)S(1)}, u32[]{:S(2)}, u32[]{:S(2)}) collective-permute-start(bf16[2,16,1536]{2,1,0:T(8,128)(2,1)S(1)} %get-tuple-element.159), channel_id=1, source_target_pairs={{1,0},{2,1},{3,2},{4,3},{5,4},{6,5},{7,6},{8,7},{9,8},{10,9},{11,1... | collective-permute-start | bytes 294920 | tf_op jit(solution)/shard_map/ppermute | solution.py:386
  104.7 15.1 %copy-start.51 = (f32[2,64]{1,0:T(2,128)}, f32[2,64]{1,0:T(2,128)S(1)}, u32[]{:S(2)}) copy-start(f32[2,64]{1,0:T(2,128)S(1)} %compare_convert_fusion) | copy-start | bytes 1540
  110.0 1.4 collective-permute-start.5
  110.1 21.0 %copy-start.55 = (f32[2,96]{1,0:T(2,128)}, f32[2,96]{1,0:T(2,128)S(1)}, u32[]{:S(2)}) copy-start(f32[2,96]{1,0:T(2,128)S(1)} %compare_convert_fusion.1) | copy-start | bytes 2308
  116.3 3.6 %copy-start.18 = (f32[1536]{0:T(1024)S(1)}, f32[1536]{0:T(1024)}, u32[]{:S(2)}) copy-start(f32[1536]{0:T(1024)} %param.15) | copy-start | bytes 18436
  119.6 1.3 copy-start.49
  119.9 1.0 copy-start.53
  120.2 12.0 %copy-start = (bf16[2,64,1536]{2,1,0:T(8,128)(2,1)S(1)}, bf16[2,64,1536]{2,1,0:T(8,128)(2,1)}, u32[]{:S(2)}) copy-start(bf16[2,64,1536]{2,1,0:T(8,128)(2,1)} %unpack.2) | copy-start | bytes 1179652
  120.9 14.1 %collective-permute-start.6 = (bf16[2,32,1536]{2,1,0:T(8,128)(2,1)}, bf16[2,32,1536]{2,1,0:T(8,128)(2,1)S(1)}, u32[]{:S(2)}, u32[]{:S(2)}) collective-permute-start(bf16[2,32,1536]{2,1,0:T(8,128)(2,1)} %get-tuple-element.154), channel_id=1, source_target_pairs={{0,1},{1,2},{2,3},{3,4},{4,5},{5,6},{6,7},{7,8},{8,9},{9,10},{10,1... | collective-permute-start | bytes 589832 | tf_op jit(solution)/shard_map/ppermute | solution.py:385
  123.7 11.5 %collective-permute-start.7 = (bf16[2,32,1536]{2,1,0:T(8,128)(2,1)S(1)}, bf16[2,32,1536]{2,1,0:T(8,128)(2,1)S(1)}, u32[]{:S(2)}, u32[]{:S(2)}) collective-permute-start(bf16[2,32,1536]{2,1,0:T(8,128)(2,1)S(1)} %get-tuple-element.155), channel_id=1, source_target_pairs={{1,0},{2,1},{3,2},{4,3},{5,4},{6,5},{7,6},{8,7},{9,8},{10,9},{11,1... | collective-permute-start | bytes 589832 | tf_op jit(solution)/shard_map/ppermute | solution.py:386
  134.7 0.8 copy-start.34
  134.7 0.8 copy-start.35
  134.8 0.8 copy-start.36
  134.8 0.8 copy-start.37
  134.8 0.8 copy-start.38
  134.8 0.8 copy-start.39
  134.8 0.8 copy-start.40
  134.8 0.8 copy-start.41
  134.8 0.8 copy-start.42
  134.8 0.8 copy-start.43
  134.8 0.8 copy-start.44
  134.8 0.8 copy-start.45
  134.9 0.8 copy-start.46
  134.9 0.8 copy-start.47
  134.9 33.0 %collective-permute-start.10 = (bf16[128,768]{0,1:T(8,128)(2,1)S(1)}, bf16[128,768]{0,1:T(8,128)(2,1)S(1)}, u32[]{:S(2)}, u32[]{:S(2)}) collective-permute-start(bf16[128,768]{0,1:T(8,128)(2,1)S(1)} %bitcast.73), channel_id=1, source_target_pairs={{0,64},{64,0},{1,65},{65,1},{2,66},{66,2},{3,67},{67,3},{4,68},{68... | collective-permute-start | bytes 589832 | tf_op jit(solution)/shard_map/ppermute | solution.py:425
  141.8 1.3 copy-start.50
  141.8 1.3 copy-start.52
  141.8 1.3 copy-start.54
  141.8 7.1 %slice-start = ((s8[4718592]{0:T(1024)(128)(4,1)}), s8[4194304]{0:T(1024)(128)(4,1)S(1)}, s32[]{:S(2)}) async-start(s8[4718592]{0:T(1024)(128)(4,1)} %bitcast.51), calls=%async_computation.8 | async-start | bytes 8388608
  143.2 5.3 %copy-start.1 = (f32[2,96,1536]{2,1,0:T(8,128)S(1)}, f32[2,96,1536]{2,1,0:T(8,128)}, u32[]{:S(2)}) copy-start(f32[2,96,1536]{2,1,0:T(8,128)} %convert_multiply_fusion) | copy-start | bytes 3538948
  143.2 5.8 %slice-start.1 = ((s8[4718592]{0:T(1024)(128)(4,1)}), s8[524288]{0:T(1024)(128)(4,1)S(1)}, s32[]{:S(2)}) async-start(s8[4718592]{0:T(1024)(128)(4,1)} %bitcast.51), calls=%async_computation.9 | async-start | bytes 1048576
  155.4 2.7 copy-start.15
  155.4 2.7 collective-permute-start.8
  156.6 11.3 %collective-permute-start.11 = (bf16[128,1536]{1,0:T(8,128)(2,1)S(1)}, bf16[128,1536]{1,0:T(8,128)(2,1)S(1)}, u32[]{:S(2)}, u32[]{:S(2)}) collective-permute-start(bf16[128,1536]{1,0:T(8,128)(2,1)S(1)} %bitcast.55), channel_id=1, source_target_pairs={{0,64},{64,0},{1,65},{65,1},{2,66},{66,2},{3,67},{67,3},{4,68},{68... | collective-permute-start | bytes 1179656 | tf_op jit(solution)/shard_map/ppermute | solution.py:426
  157.7 10.2 %collective-permute-start.12 = (f32[32,1536]{1,0:T(8,128)S(1)}, f32[32,1536]{1,0:T(8,128)S(1)}, u32[]{:S(2)}, u32[]{:S(2)}) collective-permute-start(f32[32,1536]{1,0:T(8,128)S(1)} %concatenate.47), channel_id=1, source_target_pairs={{0,64},{64,0},{1,65},{65,1},{2,66},{66,2},{3,67},{67,3},{4,68},{68... | collective-permute-start | bytes 589832 | tf_op jit(solution)/shard_map/ppermute | solution.py:427
  158.1 9.8 %copy-start.4 = (bf16[128,2,1,384]{0,3,1,2:T(8,128)(2,1)S(1)}, bf16[128,2,1,384]{0,3,1,2:T(8,128)(2,1)}, u32[]{:S(2)}) copy-start(bf16[128,2,1,384]{0,3,1,2:T(8,128)(2,1)} %copy.39) | copy-start | bytes 589828
  158.9 25.6 %all-to-all-start.2 = ((bf16[64,24,128]{2,1,0:T(8,128)(2,1)}), bf16[64,24,128]{2,1,0:T(8,128)(2,1)S(1)}, u32[]{:S(2)}, u32[]{:S(2)}) async-start(bf16[64,24,128]{2,1,0:T(8,128)(2,1)} %pad_maximum_fusion.3), calls=%async_computation.2 | async-start | bytes 786432 | tf_op jit(solution)/shard_map/all_to_all | solution.py:404
  185.3 42.3 %all-to-all-start.3 = ((bf16[16,52,1536]{2,1,0:T(8,128)(2,1)}), bf16[16,52,1536]{2,1,0:T(8,128)(2,1)S(1)}, u32[]{:S(2)}, u32[]{:S(2)}) async-start(bf16[16,52,1536]{2,1,0:T(8,128)(2,1)} %pad_maximum_fusion), calls=%async_computation.3 | async-start | bytes 5505024 | tf_op jit(solution)/shard_map/all_to_all | solution.py:438
  222.3 13.4 %collective-permute-start.9 = (bf16[64,48,128]{2,1,0:T(8,128)(2,1)}, bf16[64,48,128]{2,1,0:T(8,128)(2,1)}, u32[]{:S(2)}, u32[]{:S(2)}) collective-permute-start(bf16[64,48,128]{2,1,0:T(8,128)(2,1)} %get-tuple-element.46), channel_id=1, source_target_pairs={{0,64},{64,0},{1,65},{65,1},{2,66},{66,2},{3,67},{67,3},{4,68},{68... | collective-permute-start | bytes 2359304 | tf_op jit(solution)/shard_map/ppermute | solution.py:539
  228.7 7.0 %copy-start.2 = (f32[64,48,128]{2,1,0:T(8,128)S(1)}, f32[64,48,128]{2,1,0:T(8,128)}, u32[]{:S(2)}) copy-start(f32[64,48,128]{2,1,0:T(8,128)} %get-tuple-element.45) | copy-start | bytes 4718596
  231.5 17.4 %all-to-all-start.4 = ((bf16[8,10,1536]{2,1,0:T(8,128)(2,1)}), bf16[8,10,1536]{2,1,0:T(8,128)(2,1)S(1)}, u32[]{:S(2)}, u32[]{:S(2)}) async-start(bf16[8,10,1536]{2,1,0:T(8,128)(2,1)} %pad_maximum_fusion.4), calls=%async_computation.4 | async-start | bytes 786432 | tf_op jit(solution)/shard_map/all_to_all | solution.py:442
  235.7 1.4 copy-start.6
  237.1 11.8 %copy-start.58 = (pred[8]{0:T(512)(128)(4,1)S(1)}, pred[8]{0:T(512)(128)(4,1)}, u32[]{:S(2)}) copy-start(pred[8]{0:T(512)(128)(4,1)} %constant.86.clone.1) | copy-start | bytes 28
  249.0 53.0 %all-to-all-start.5 = ((bf16[64,72,128]{2,1,0:T(8,128)(2,1)}), bf16[64,72,128]{2,1,0:T(8,128)(2,1)S(1)}, u32[]{:S(2)}, u32[]{:S(2)}) async-start(bf16[64,72,128]{2,1,0:T(8,128)(2,1)} %pad_maximum_fusion.2), calls=%async_computation.5 | async-start | bytes 2359296 | tf_op jit(solution)/shard_map/all_to_all | solution.py:408
  303.2 20.4 %all-to-all-start.6 = ((bf16[8,56,1536]{2,1,0:T(8,128)(2,1)}), bf16[8,56,1536]{2,1,0:T(8,128)(2,1)S(1)}, u32[]{:S(2)}, u32[]{:S(2)}) async-start(bf16[8,56,1536]{2,1,0:T(8,128)(2,1)} %broadcast_in_dim.11), calls=%async_computation.6 | async-start | bytes 2752512 | tf_op jit(solution)/shard_map/all_to_all | solution.py:453
  309.9 2.5 collective-permute-start.13
  312.4 0.8 copy-start.5
  318.2 4.3 %copy-start.10 = (bf16[2,64,1536]{2,1,0:T(8,128)(2,1)S(1)}, bf16[2,64,1536]{2,1,0:T(8,128)(2,1)}, u32[]{:S(2)}) copy-start(bf16[2,64,1536]{2,1,0:T(8,128)(2,1)} %get-tuple-element.52) | copy-start | bytes 1179652
  324.1 2.4 copy-start.14
  (19 other events, 14.7 us)
Sparse Core Ops, SparseCore 0:
  9.8 58.6 all-gather.1
where the time goes:
time: 339 us; the launch traced here: 334 us
  blocking collectives  92.3 us (27%)
  Pallas kernels  65.8 us (19%)
  starting transfers between devices  59.5 us (18%)
  waiting for transfers between devices  41 us (12%)
  local copies, waits for them, and re-layouts  26.6 us (8%)
  other arithmetic  26.3 us (8%)
  between operations  15.5 us (5%)
  matrix products  6.49 us (2%)
    all_gather x1, blocking collectives, per_device(): rows = lax.all_gather(rows, 'z', axis=0, tiled=True)  46.8 us
    all_to_all x1, blocking collectives, to_pairs(): return lax.all_to_all(in_order(core, mine, theirs), SEQ, 0, 0, tiled=True)  45.5 us
    pallas_call x1, Pallas kernels, attend_back(): pl.pallas_call(backward_kernel, out_shape=(jax.ShapeDtypeStruct((sources,...  30.9 us
    pallas_call x1, Pallas kernels, attend(): pl.pallas_call(forward_kernel, out_shape=(jax.ShapeDtypeStruct((sources,...  16.9 us
    ppermute x2, starting transfers between devices, with_halo(): after = lax.ppermute(shard[:, :width], SEQ, down)  14.4 us
    unnamed x133, local copies, waits for them, and re-layouts  14 us
    all_to_all x1, waiting for transfers between devices, to_pairs(): return lax.all_to_all(in_order(core, mine, theirs), SEQ, 0, 0, tiled=True)  13.9 us
    all_to_all x2, starting transfers between devices, exchange(): return lax.all_to_all(blocks, SEQ, 0, 0, tiled=True)  11.9 us
  transfers between devices with their start and end apart: 21, of which 8 were waited for; matrix products, arithmetic and copies ran while one was open for 15% of the time, Pallas kernels for 20%

commit v1 on v0

--- a/solution.py
+++ b/solution.py
@@ -80,7 +80,7 @@
                 target[index * 4 + head] = jnp.concatenate(slab).astype(BF16)
             return carry
 
-        lax.fori_loop(0, 8, step, 0)
+        lax.fori_loop(0, 8, step, 0, unroll=8 if len(sources) == 1 else 1)
 
 
 def pack(core, *sources):
@@ -121,7 +121,7 @@
                 target[utterance, pl.ds(start, HALF), columns] = wide
             return carry
 
-        lax.fori_loop(0, 8, step, 0)
+        lax.fori_loop(0, 8, step, 0, unroll=8 if len(targets) == 1 else 1)
 
 
 def unpack(core, mine, theirs):
@@ -401,7 +401,7 @@
 def to_pairs(core, *sources):
     mine, theirs = pack(core[None], *sources)
     theirs = lax.ppermute(theirs, "c", SWAP)
-    return lax.all_to_all(in_order(core, mine, theirs), SEQ, 0, 0, tiled=True)
+    return in_order(core, mine, theirs)
 
 
 def exchange(blocks):
@@ -478,7 +478,10 @@
         return tensor.transpose(1, 0, 2)
 
     wide_cotangent = with_halo(turned(cotangent), RIM)
-    own = to_pairs(core, turned(query_proj), turned(key_proj), turned(value_proj))
+    own, info = lax.optimization_barrier(
+        (to_pairs(core, turned(query_proj), turned(key_proj), turned(value_proj)), info)
+    )
+    own = exchange(own)
     other = lax.ppermute(own, "c", SWAP)
     mixed, output, plain, query, key, value = attend(info, own, other)
     (attention,) = to_frames(core, exchange(mixed))
@@ -530,7 +533,7 @@
         flat_grad, weight, (((1,), (1,)), ((), ())), preferred_element_type=F32
     )
     grad_attention = grad_flat.astype(BF16).reshape(utterances, frames, width)
-    head_grad = to_pairs(core, grad_attention)
+    head_grad = exchange(to_pairs(core, grad_attention))
     rows, small = sum_parameters(flat_attn, flat_grad, small)
     head_grad, block_out, grad_input = lax.optimization_barrier(
         (head_grad, turned(block_out), turned(grad_input))

time: 339 us -> 336 us (level)
    all_to_all x1 -> x0, waiting for transfers between devices: 13.9 us -> none  [to_pairs(): return lax.all_to_all(in_order(core, mine, theirs), SEQ, 0, 0, tiled=True)]
    all_to_all x2 -> x3, waiting for transfers between devices: 4.52 us -> 18.3 us  [exchange(): return lax.all_to_all(blocks, SEQ, 0, 0, tiled=True)]
    all_to_all x2 -> x3, starting transfers between devices: 11.9 us -> 21 us  [exchange(): return lax.all_to_all(blocks, SEQ, 0, 0, tiled=True)]
    all_to_all x1 -> x0, starting transfers between devices: 8.89 us -> none  [to_pairs(): return lax.all_to_all(in_order(core, mine, theirs), SEQ, 0, 0, tiled=True)]
  transfers between devices with their start and end apart: 21 -> 21, of which waited for: 8 -> 8; matrix products, arithmetic and copies ran while one was open for 15% -> 16% of each run, Pallas kernels for 20% -> 19%
where the time goes in v1:
time: 336 us; the launch traced here: 330 us
  blocking collectives  92.3 us (27%)
  Pallas kernels  62.7 us (19%)
  starting transfers between devices  60 us (18%)
  waiting for transfers between devices  40.3 us (12%)
  local copies, waits for them, and re-layouts  26.6 us (8%)
  other arithmetic  26.3 us (8%)
  between operations  15.5 us (5%)
  matrix products  6.51 us (2%)
    all_gather x1, blocking collectives, per_device(): rows = lax.all_gather(rows, 'z', axis=0, tiled=True)  46.8 us
    all_to_all x1, blocking collectives, exchange(): return lax.all_to_all(blocks, SEQ, 0, 0, tiled=True)  45.5 us
    pallas_call x1, Pallas kernels, attend_back(): pl.pallas_call(backward_kernel, out_shape=(jax.ShapeDtypeStruct((sources,...  31 us
    all_to_all x3, starting transfers between devices, exchange(): return lax.all_to_all(blocks, SEQ, 0, 0, tiled=True)  21 us
    all_to_all x3, waiting for transfers between devices, exchange(): return lax.all_to_all(blocks, SEQ, 0, 0, tiled=True)  18.3 us
    pallas_call x1, Pallas kernels, attend(): pl.pallas_call(forward_kernel, out_shape=(jax.ShapeDtypeStruct((sources,...  16.9 us
    ppermute x2, starting transfers between devices, with_halo(): after = lax.ppermute(shard[:, :width], SEQ, down)  14.2 us
    unnamed x133, local copies, waits for them, and re-layouts  14 us
  transfers between devices with their start and end apart: 21, of which 8 were waited for; matrix products, arithmetic and copies ran while one was open for 16% of the time, Pallas kernels for 19%

profile of v1, /device:TPU:8, one launch (start us, length us, event | category | flops | bytes accessed | tf_op | source)
XLA Modules:
  0.0 330.4 jit_solution(17345240697633019379)
XLA Ops:
  7.2 0.7 all-gather.2.cloned.1.call-update
  8.3 1.0 copy_bitcast_fusion
  9.3 0.8 copy.46
  10.0 4.8 %pack.2 = (bf16[32,72,128]{2,1,0:T(8,128)(2,1)}, bf16[32,72,128]{2,1,0:T(8,128)(2,1)}) custom-call(s32[1]{0:T(128)} %bitcast.core_ref, bf16[2,64,1536]{2,1,0:T(8,128)(2,1)} %bitcast.64, bf16[2,64,1536]{2,1,0:T(8,128)(2,1)} %get-tuple-element.169.refs_1_, bf16[2,64,1536]{2,1,0:T(8,128)(2,1)} %get-tuple-element.168.refs_2_), custom_call_target="tpu_custom_call" | custom-call | bytes 25165824 | tf_op jit(solution)/shard_map/pack/pallas_call | solution.py:88
  15.3 1.1 collective-permute-done.3
  17.1 1.2 pad_add_fusion.1.info_ref
  18.4 1.1 broadcast_select_fusion.1
  19.6 45.5 %all_to_all.35.own_ref = bf16[64,72,128]{2,1,0:T(8,128)(2,1)S(1)} all-to-all(bf16[64,72,128]{2,1,0:T(8,128)(2,1)S(1)} %pad_maximum_fusion.1), channel_id=1, replica_groups=mesh['yh'=2,'c'=2,'yl'=2,'x'=4,'z'=8] {'yl','x','z'}, dimensions={0} | all-to-all | bytes 2359296 | tf_op jit(solution)/shard_map/all_to_all | solution.py:408
  65.4 2.8 collective-permute-done.4.other_ref
  68.2 1.0 copy-done.59
  69.2 16.9 %attend.1 = (bf16[64,24,128]{2,1,0:T(8,128)(2,1)}, f32[2048,128]{1,0:T(8,128)}, bf16[2048,128]{1,0:T(8,128)(2,1)}, bf16[2048,256]{1,0:T(8,128)(2,1)}, bf16[4096,...) custom-call(s32[2]{0:T(128)} %pad_add_fusion.1.info_ref, bf16[64,72,128]{2,1,0:T(8,128)(2,1)} %copy-done.3, ...), custom_call_target="tpu_custom_call" | custom-call | flops 8589934592 | bytes 8388608 | tf_op jit(solution)/shard_map/attend/pallas_call | solution.py:268
  86.1 6.0 %all-to-all-start.1 = ((bf16[64,24,128]{2,1,0:T(8,128)(2,1)}), bf16[64,24,128]{2,1,0:T(8,128)(2,1)S(1)}, u32[]{:S(2)}, u32[]{:S(2)}) async-start(bf16[64,24,128]{2,1,0:T(8,128)(2,1)} %get-tuple-element.37), calls=%async_computation.1 | async-start | bytes 786432 | tf_op jit(solution)/shard_map/all_to_all | solution.py:408
  92.1 3.5 %collective-permute-start = (bf16[2,16,1536]{2,1,0:T(8,128)(2,1)S(1)}, bf16[2,16,1536]{2,1,0:T(8,128)(2,1)S(1)}, u32[]{:S(2)}, u32[]{:S(2)}) collective-permute-start(bf16[2,16,1536]{2,1,0:T(8,128)(2,1)S(1)} %get-tuple-element.162), channel_id=1, source_target_pairs={{0,1},{1,2},{2,3},{3,4},{4,5},{5,6},{6,7},{7,8},{8,9},{9,10},{10,1... | collective-permute-start | bytes 294920 | tf_op jit(solution)/shard_map/ppermute | solution.py:385
  95.7 7.1 %collective-permute-start.1 = (bf16[2,16,1536]{2,1,0:T(8,128)(2,1)S(1)}, bf16[2,16,1536]{2,1,0:T(8,128)(2,1)S(1)}, u32[]{:S(2)}, u32[]{:S(2)}) collective-permute-start(bf16[2,16,1536]{2,1,0:T(8,128)(2,1)S(1)} %get-tuple-element.163), channel_id=1, source_target_pairs={{1,0},{2,1},{3,2},{4,3},{5,4},{6,5},{7,6},{8,7},{9,8},{10,9},{11,1... | collective-permute-start | bytes 294920 | tf_op jit(solution)/shard_map/ppermute | solution.py:386
  102.8 0.8 slice_reduce_fusion.30
  103.6 0.9 slice_reduce_fusion.31
  104.6 4.3 %all-to-all-done.1 = bf16[64,24,128]{2,1,0:T(8,128)(2,1)S(1)} async-done(((bf16[64,24,128]{2,1,0:T(8,128)(2,1)}), bf16[64,24,128]{2,1,0:T(8,128)(2,1)S(1)}, u32[]{:S(2)}, u32[]{:S(2)}) %all-to-all-start.1) | async-done | bytes 393248 | tf_op jit(solution)/shard_map/all_to_all | solution.py:408
  108.9 0.7 dynamic-slice_bitcast_fusion.2
  109.7 1.4 collective-permute-done.5.theirs_ref
  111.7 2.6 unpack.2
  114.3 3.4 %fusion.111 = (f32[2,64]{1,0:T(2,128)S(1)}, f32[2,64,1536]{2,1,0:T(8,128)S(1)}) fusion(bf16[2,64,1536]{2,1,0:T(8,128)(2,1)} %unpack.2, bf16[1536,1536]{1,0:T(8,128)(2,1)} %all-gather.2.cloned.1.call-done, bf16[64,2,1536]{2,1,0:T(2,128)(2,1)S(1)} %copy-done.13), kind=kOutput, calls=%fused_computation.284 | convolution fusion | flops 604569472 | bytes 6291968 | tf_op jit(solution)/shard_map/dot_general | solution.py:489
  118.3 0.7 fusion.109
  119.0 2.9 collective-permute-start.6
  122.0 7.1 %collective-permute-start.7 = (bf16[2,32,1536]{2,1,0:T(8,128)(2,1)S(1)}, bf16[2,32,1536]{2,1,0:T(8,128)(2,1)S(1)}, u32[]{:S(2)}, u32[]{:S(2)}) collective-permute-start(bf16[2,32,1536]{2,1,0:T(8,128)(2,1)S(1)} %get-tuple-element.159), channel_id=1, source_target_pairs={{1,0},{2,1},{3,2},{4,3},{5,4},{6,5},{7,6},{8,7},{9,8},{10,9},{11,1... | collective-permute-start | bytes 589832 | tf_op jit(solution)/shard_map/ppermute | solution.py:386
  129.1 1.2 convert_multiply_fusion
  130.4 0.8 constant_dynamic-slice_fusion.1
  131.2 1.0 copy.39
  133.8 5.2 %fusion.101 = (f32[2,96,1536]{2,1,0:T(8,128)S(1)}, f32[2,96,1536]{2,1,0:T(8,128)S(1)}) fusion(f32[2,96]{1,0:T(2,128)S(1)} %copy-done.56, bf16[2,16,1536]{2,1,0:T(8,128)(2,1)S(1)} %collective-permute-done.1, bf16[2,64,1536]{2,1,0:T(8,128)(2,1)S(1)} %bitcast.60, bf16[2,16,1536]{2,1,0:T(8,128)(2,1)S(1)} %collective-permute-done, ...), kind=kLoop, calls=%fused_computation.211 | loop fusion | flops 23003136 | bytes 39709440 | tf_op jit(solution)/shard_map/convert_element_type | solution.py:509
  138.9 0.9 fusion.52
  139.9 1.3 fusion.43
  141.2 5.3 %multiply_reduce_fusion = (f32[1536]{0:T(1024)S(1)}, f32[2,64]{1,0:T(2,128)S(1)}, f32[2,64]{1,0:T(2,128)S(1)}, f32[2,64,1536]{2,1,0:T(8,128)S(1)}) fusion(f32[2,64,1536]{2,1,0:T(8,128)S(1)} %get-tuple-element.167, f32[2,64]{1,0:T(2,128)S(1)} %copy-done.54, f32[2,64]{1,0:T(2,128)S(1)} %copy-done.50, f32[1536]{0:T(1024)S(1)} %copy-done.18, ...), kind=kLoop, calls=%fused_computation.202 | loop fusion | flops 13760768 | bytes 26157568 | tf_op jit(solution)/shard_map/reduce_sum | solution.py:519
  147.0 2.4 convolution_convert_fusion.1
  149.4 2.5 pack.3
  152.2 0.9 fusion.35
  154.7 0.8 pad_maximum_fusion.3
  155.5 8.9 %all-to-all-start.2 = ((bf16[64,24,128]{2,1,0:T(8,128)(2,1)}), bf16[64,24,128]{2,1,0:T(8,128)(2,1)S(1)}, u32[]{:S(2)}, u32[]{:S(2)}) async-start(bf16[64,24,128]{2,1,0:T(8,128)(2,1)} %pad_maximum_fusion.3), calls=%async_computation.2 | async-start | bytes 786432 | tf_op jit(solution)/shard_map/all_to_all | solution.py:408
  164.5 0.8 convolution_convert_fusion
  165.3 1.8 pad_maximum_fusion
  167.1 13.9 %all-to-all-done.2.grad_ref = bf16[64,24,128]{2,1,0:T(8,128)(2,1)S(1)} async-done(((bf16[64,24,128]{2,1,0:T(8,128)(2,1)}), bf16[64,24,128]{2,1,0:T(8,128)(2,1)S(1)}, u32[]{:S(2)}, u32[]{:S(2)}) %all-to-all-start.2) | async-done | bytes 393248 | tf_op jit(solution)/shard_map/all_to_all | solution.py:408
  181.1 0.7 copy-done.9
  181.8 6.3 %all-to-all-start.3 = ((bf16[16,52,1536]{2,1,0:T(8,128)(2,1)}), bf16[16,52,1536]{2,1,0:T(8,128)(2,1)S(1)}, u32[]{:S(2)}, u32[]{:S(2)}) async-start(bf16[16,52,1536]{2,1,0:T(8,128)(2,1)} %pad_maximum_fusion), calls=%async_computation.3 | async-start | bytes 5505024 | tf_op jit(solution)/shard_map/all_to_all | solution.py:438
  188.2 31.0 %attend_back.1 = (bf16[64,24,128]{2,1,0:T(8,128)(2,1)}, f32[64,48,128]{2,1,0:T(8,128)}, bf16[64,48,128]{2,1,0:T(8,128)(2,1)}) custom-call(bf16[64,24,128]{2,1,0:T(8,128)(2,1)} %copy-done.9, f32[2048,128]{1,0:T(8,128)} %get-tuple-element.43.output_ref, bf16[2048,128]{1,0:T(8,128)(2,1)} %get-tuple-element.44.plain_ref, ...), custom_call_target="tpu_custom_call" | custom-call | flops 21474836480 | bytes 8388608 | tf_op jit(solution)/shard_map/attend_back/pallas_call | solution.py:361
  219.1 5.3 %all-to-all-done.3 = bf16[16,52,1536]{2,1,0:T(8,128)(2,1)S(1)} async-done(((bf16[16,52,1536]{2,1,0:T(8,128)(2,1)}), bf16[16,52,1536]{2,1,0:T(8,128)(2,1)S(1)}, u32[]{:S(2)}, u32[]{:S(2)}) %all-to-all-start.3) | async-done | bytes 2555936 | tf_op jit(solution)/shard_map/all_to_all | solution.py:438
  224.4 1.1 reduce_sum.381
  225.6 0.9 slice.694
  226.4 0.9 slice.693
  227.4 0.9 pad_maximum_fusion.4
  228.3 4.2 %all-to-all-start.4 = ((bf16[8,10,1536]{2,1,0:T(8,128)(2,1)}), bf16[8,10,1536]{2,1,0:T(8,128)(2,1)S(1)}, u32[]{:S(2)}, u32[]{:S(2)}) async-start(bf16[8,10,1536]{2,1,0:T(8,128)(2,1)} %pad_maximum_fusion.4), calls=%async_computation.4 | async-start | bytes 786432 | tf_op jit(solution)/shard_map/all_to_all | solution.py:442
  232.6 1.3 add_convert_fusion
  233.9 1.1 pad_maximum_fusion.2
  235.0 10.6 %all-to-all-done.4 = bf16[8,10,1536]{2,1,0:T(8,128)(2,1)S(1)} async-done(((bf16[8,10,1536]{2,1,0:T(8,128)(2,1)}), bf16[8,10,1536]{2,1,0:T(8,128)(2,1)S(1)}, u32[]{:S(2)}, u32[]{:S(2)}) %all-to-all-start.4) | async-done | bytes 245792 | tf_op jit(solution)/shard_map/all_to_all | solution.py:442
  245.8 6.1 %all-to-all-start.5 = ((bf16[64,72,128]{2,1,0:T(8,128)(2,1)}), bf16[64,72,128]{2,1,0:T(8,128)(2,1)S(1)}, u32[]{:S(2)}, u32[]{:S(2)}) async-start(bf16[64,72,128]{2,1,0:T(8,128)(2,1)} %pad_maximum_fusion.2), calls=%async_computation.5 | async-start | bytes 2359296 | tf_op jit(solution)/shard_map/all_to_all | solution.py:408
  252.0 46.8 %all_gather.7 = bf16[64,1536]{1,0:T(8,128)(2,1)S(1)} all-gather(bf16[8,1536]{1,0:T(8,128)(2,1)S(1)} %slice_select_fusion), channel_id=1, replica_groups=mesh['yh'=2,'c'=2,'yl'=2,'x'=4,'z'=8] {'z'}, dimensions={0}, use_global_device_ids=true | all-gather | bytes 221184 | tf_op jit(solution)/shard_map/all_gather | solution.py:547
  298.9 1.2 broadcast_in_dim.11
  300.1 5.8 %all-to-all-start.6 = ((bf16[8,56,1536]{2,1,0:T(8,128)(2,1)}), bf16[8,56,1536]{2,1,0:T(8,128)(2,1)S(1)}, u32[]{:S(2)}, u32[]{:S(2)}) async-start(bf16[8,56,1536]{2,1,0:T(8,128)(2,1)} %broadcast_in_dim.11), calls=%async_computation.6 | async-start | bytes 2752512 | tf_op jit(solution)/shard_map/all_to_all | solution.py:453
  305.9 0.9 dynamic-slice_bitcast_fusion
  307.0 1.2 copy.34
  308.1 1.1 copy.35
  309.3 0.8 copy-done.5
  310.1 4.9 %unpack.3 = (bf16[2,64,1536]{2,1,0:T(8,128)(2,1)}, bf16[2,64,1536]{2,1,0:T(8,128)(2,1)}, bf16[2,64,1536]{2,1,0:T(8,128)(2,1)}) custom-call(s32[1]{0:T(128)} %bitcast.core_ref, bf16[32,72,128]{2,1,0:T(8,128)(2,1)} %get-tuple-element.149.mine_ref, bf16[32,72,128]{2,1,0:T(8,128)(2,1)} %copy-done.5), custom_call_target="tpu_custom_call" | custom-call | bytes 25165824 | tf_op jit(solution)/shard_map/unpack/pallas_call | solution.py:130
  315.0 2.2 copy.36
  317.2 2.1 copy.37
  319.3 1.2 copy.38
  321.6 1.7 slice.698
  (215 shorter events, 8.4 us)
Async XLA Ops:
  7.2 1.0 copy-start.11
  7.2 1.1 copy-start.12
  7.2 2.1 copy-start.7
  7.2 107.1 %all-gather.2.cloned.1.call-start = ((), (), s32[]{:S(2)}) async-start(), calls=%async_computation.7 | async-start | bytes 5898240 | tf_op jit(solution)/shard_map/all_gather | solution.py:475
  9.2 5.6 %copy-start.57 = (s32[2]{0:T(128)S(1)}, s32[2]{0:T(128)}, u32[]{:S(2)}) copy-start(s32[2]{0:T(128)} %param.13) | copy-start | bytes 28
  14.8 3.5 %collective-permute-start.2 = (bf16[32,72,128]{2,1,0:T(8,128)(2,1)}, bf16[32,72,128]{2,1,0:T(8,128)(2,1)S(1)}, u32[]{:S(2)}, u32[]{:S(2)}) collective-permute-start(bf16[32,72,128]{2,1,0:T(8,128)(2,1)} %get-tuple-element.34), channel_id=1, source_target_pairs={{0,64},{64,0},{1,65},{65,1},{2,66},{66,2},{3,67},{67,3},{4,68},{68... | collective-permute-start | bytes 1769480 | tf_op jit(solution)/shard_map/ppermute | solution.py:403
  14.8 1.6 collective-permute-start.3
  19.6 45.7 %copy-start.8 = (bf16[64,2,1536]{2,1,0:T(2,128)(2,1)S(1)}, bf16[64,2,1536]{2,1,0:T(2,128)(2,1)}, u32[]{:S(2)}) copy-start(bf16[64,2,1536]{2,1,0:T(2,128)(2,1)} %param.17) | copy-start | bytes 1179652
  65.2 3.0 copy-start.3
  65.2 3.0 collective-permute-start.4
  68.2 1.0 copy-start.59
  86.1 16.7 %copy-start.17 = (f32[31,1536]{1,0:T(8,128)S(1)}, f32[31,1536]{1,0:T(8,128)}, u32[]{:S(2)}) copy-start(f32[31,1536]{1,0:T(8,128)} %param.16) | copy-start | bytes 571396
  86.1 22.7 %all-to-all-start.1 = ((bf16[64,24,128]{2,1,0:T(8,128)(2,1)}), bf16[64,24,128]{2,1,0:T(8,128)(2,1)S(1)}, u32[]{:S(2)}, u32[]{:S(2)}) async-start(bf16[64,24,128]{2,1,0:T(8,128)(2,1)} %get-tuple-element.37), calls=%async_computation.1 | async-start | bytes 786432 | tf_op jit(solution)/shard_map/all_to_all | solution.py:408
  92.1 22.2 %copy-start.13 = (bf16[64,2,1536]{2,1,0:T(2,128)(2,1)S(1)}, bf16[64,2,1536]{2,1,0:T(2,128)(2,1)}, u32[]{:S(2)}) copy-start(bf16[64,2,1536]{2,1,0:T(2,128)(2,1)} %param.9) | copy-start | bytes 1179652
  92.1 36.9 %collective-permute-start = (bf16[2,16,1536]{2,1,0:T(8,128)(2,1)S(1)}, bf16[2,16,1536]{2,1,0:T(8,128)(2,1)S(1)}, u32[]{:S(2)}, u32[]{:S(2)}) collective-permute-start(bf16[2,16,1536]{2,1,0:T(8,128)(2,1)S(1)} %get-tuple-element.162), channel_id=1, source_target_pairs={{0,1},{1,2},{2,3},{3,4},{4,5},{5,6},{6,7},{7,8},{8,9},{9,10},{10,1... | collective-permute-start | bytes 294920 | tf_op jit(solution)/shard_map/ppermute | solution.py:385
  95.7 33.4 %collective-permute-start.1 = (bf16[2,16,1536]{2,1,0:T(8,128)(2,1)S(1)}, bf16[2,16,1536]{2,1,0:T(8,128)(2,1)S(1)}, u32[]{:S(2)}, u32[]{:S(2)}) collective-permute-start(bf16[2,16,1536]{2,1,0:T(8,128)(2,1)S(1)} %get-tuple-element.163), channel_id=1, source_target_pairs={{1,0},{2,1},{3,2},{4,3},{5,4},{6,5},{7,6},{8,7},{9,8},{10,9},{11,1... | collective-permute-start | bytes 294920 | tf_op jit(solution)/shard_map/ppermute | solution.py:386
  104.6 13.4 %copy-start.51 = (f32[2,64]{1,0:T(2,128)}, f32[2,64]{1,0:T(2,128)S(1)}, u32[]{:S(2)}) copy-start(f32[2,64]{1,0:T(2,128)S(1)} %compare_convert_fusion) | copy-start | bytes 1540
  109.6 1.4 collective-permute-start.5
  109.7 19.4 %copy-start.55 = (f32[2,96]{1,0:T(2,128)}, f32[2,96]{1,0:T(2,128)S(1)}, u32[]{:S(2)}) copy-start(f32[2,96]{1,0:T(2,128)S(1)} %compare_convert_fusion.1) | copy-start | bytes 2308
  114.3 3.6 %copy-start.18 = (f32[1536]{0:T(1024)S(1)}, f32[1536]{0:T(1024)}, u32[]{:S(2)}) copy-start(f32[1536]{0:T(1024)} %param.15) | copy-start | bytes 18436
  117.7 1.3 copy-start.49
  118.0 1.0 copy-start.53
  118.3 12.0 %copy-start = (bf16[2,64,1536]{2,1,0:T(8,128)(2,1)S(1)}, bf16[2,64,1536]{2,1,0:T(8,128)(2,1)}, u32[]{:S(2)}) copy-start(bf16[2,64,1536]{2,1,0:T(8,128)(2,1)} %unpack.2) | copy-start | bytes 1179652
  119.0 14.1 %collective-permute-start.6 = (bf16[2,32,1536]{2,1,0:T(8,128)(2,1)}, bf16[2,32,1536]{2,1,0:T(8,128)(2,1)S(1)}, u32[]{:S(2)}, u32[]{:S(2)}) collective-permute-start(bf16[2,32,1536]{2,1,0:T(8,128)(2,1)} %get-tuple-element.158), channel_id=1, source_target_pairs={{0,1},{1,2},{2,3},{3,4},{4,5},{5,6},{6,7},{7,8},{8,9},{9,10},{10,1... | collective-permute-start | bytes 589832 | tf_op jit(solution)/shard_map/ppermute | solution.py:385
  122.0 11.3 %collective-permute-start.7 = (bf16[2,32,1536]{2,1,0:T(8,128)(2,1)S(1)}, bf16[2,32,1536]{2,1,0:T(8,128)(2,1)S(1)}, u32[]{:S(2)}, u32[]{:S(2)}) collective-permute-start(bf16[2,32,1536]{2,1,0:T(8,128)(2,1)S(1)} %get-tuple-element.159), channel_id=1, source_target_pairs={{1,0},{2,1},{3,2},{4,3},{5,4},{6,5},{7,6},{8,7},{9,8},{10,9},{11,1... | collective-permute-start | bytes 589832 | tf_op jit(solution)/shard_map/ppermute | solution.py:386
  132.8 0.8 copy-start.34
  132.8 0.8 copy-start.35
  132.8 0.8 copy-start.36
  132.8 0.8 copy-start.37
  132.8 0.8 copy-start.38
  132.9 0.8 copy-start.39
  132.9 0.8 copy-start.40
  132.9 0.8 copy-start.41
  132.9 0.8 copy-start.42
  132.9 0.8 copy-start.43
  132.9 0.8 copy-start.44
  132.9 0.8 copy-start.45
  132.9 0.8 copy-start.46
  132.9 0.8 copy-start.47
  133.0 31.5 %collective-permute-start.10 = (bf16[128,768]{0,1:T(8,128)(2,1)S(1)}, bf16[128,768]{0,1:T(8,128)(2,1)S(1)}, u32[]{:S(2)}, u32[]{:S(2)}) collective-permute-start(bf16[128,768]{0,1:T(8,128)(2,1)S(1)} %bitcast.73), channel_id=1, source_target_pairs={{0,64},{64,0},{1,65},{65,1},{2,66},{66,2},{3,67},{67,3},{4,68},{68... | collective-permute-start | bytes 589832 | tf_op jit(solution)/shard_map/ppermute | solution.py:425
  139.9 1.3 copy-start.50
  139.9 1.3 copy-start.52
  139.9 1.3 copy-start.54
  139.9 7.1 %slice-start = ((s8[4718592]{0:T(1024)(128)(4,1)}), s8[4194304]{0:T(1024)(128)(4,1)S(1)}, s32[]{:S(2)}) async-start(s8[4718592]{0:T(1024)(128)(4,1)} %bitcast.51), calls=%async_computation.8 | async-start | bytes 8388608
  141.2 5.3 %copy-start.1 = (f32[2,96,1536]{2,1,0:T(8,128)S(1)}, f32[2,96,1536]{2,1,0:T(8,128)}, u32[]{:S(2)}) copy-start(f32[2,96,1536]{2,1,0:T(8,128)} %convert_multiply_fusion) | copy-start | bytes 3538948
  141.2 5.8 %slice-start.1 = ((s8[4718592]{0:T(1024)(128)(4,1)}), s8[524288]{0:T(1024)(128)(4,1)S(1)}, s32[]{:S(2)}) async-start(s8[4718592]{0:T(1024)(128)(4,1)} %bitcast.51), calls=%async_computation.9 | async-start | bytes 1048576
  151.9 2.7 copy-start.15
  151.9 2.7 collective-permute-start.8
  153.2 11.3 %collective-permute-start.11 = (bf16[128,1536]{1,0:T(8,128)(2,1)S(1)}, bf16[128,1536]{1,0:T(8,128)(2,1)S(1)}, u32[]{:S(2)}, u32[]{:S(2)}) collective-permute-start(bf16[128,1536]{1,0:T(8,128)(2,1)S(1)} %bitcast.55), channel_id=1, source_target_pairs={{0,64},{64,0},{1,65},{65,1},{2,66},{66,2},{3,67},{67,3},{4,68},{68... | collective-permute-start | bytes 1179656 | tf_op jit(solution)/shard_map/ppermute | solution.py:426
  154.2 10.1 %collective-permute-start.12 = (f32[32,1536]{1,0:T(8,128)S(1)}, f32[32,1536]{1,0:T(8,128)S(1)}, u32[]{:S(2)}, u32[]{:S(2)}) collective-permute-start(f32[32,1536]{1,0:T(8,128)S(1)} %concatenate.47), channel_id=1, source_target_pairs={{0,64},{64,0},{1,65},{65,1},{2,66},{66,2},{3,67},{67,3},{4,68},{68... | collective-permute-start | bytes 589832 | tf_op jit(solution)/shard_map/ppermute | solution.py:427
  154.7 9.8 %copy-start.4 = (bf16[128,2,1,384]{0,3,1,2:T(8,128)(2,1)S(1)}, bf16[128,2,1,384]{0,3,1,2:T(8,128)(2,1)}, u32[]{:S(2)}) copy-start(bf16[128,2,1,384]{0,3,1,2:T(8,128)(2,1)} %copy.39) | copy-start | bytes 589828
  155.5 25.6 %all-to-all-start.2 = ((bf16[64,24,128]{2,1,0:T(8,128)(2,1)}), bf16[64,24,128]{2,1,0:T(8,128)(2,1)S(1)}, u32[]{:S(2)}, u32[]{:S(2)}) async-start(bf16[64,24,128]{2,1,0:T(8,128)(2,1)} %pad_maximum_fusion.3), calls=%async_computation.2 | async-start | bytes 786432 | tf_op jit(solution)/shard_map/all_to_all | solution.py:408
  181.8 42.6 %all-to-all-start.3 = ((bf16[16,52,1536]{2,1,0:T(8,128)(2,1)}), bf16[16,52,1536]{2,1,0:T(8,128)(2,1)S(1)}, u32[]{:S(2)}, u32[]{:S(2)}) async-start(bf16[16,52,1536]{2,1,0:T(8,128)(2,1)} %pad_maximum_fusion), calls=%async_computation.3 | async-start | bytes 5505024 | tf_op jit(solution)/shard_map/all_to_all | solution.py:438
  219.1 13.4 %collective-permute-start.9 = (bf16[64,48,128]{2,1,0:T(8,128)(2,1)}, bf16[64,48,128]{2,1,0:T(8,128)(2,1)}, u32[]{:S(2)}, u32[]{:S(2)}) collective-permute-start(bf16[64,48,128]{2,1,0:T(8,128)(2,1)} %get-tuple-element.50), channel_id=1, source_target_pairs={{0,64},{64,0},{1,65},{65,1},{2,66},{66,2},{3,67},{67,3},{4,68},{68... | collective-permute-start | bytes 2359304 | tf_op jit(solution)/shard_map/ppermute | solution.py:542
  225.6 7.0 %copy-start.2 = (f32[64,48,128]{2,1,0:T(8,128)S(1)}, f32[64,48,128]{2,1,0:T(8,128)}, u32[]{:S(2)}) copy-start(f32[64,48,128]{2,1,0:T(8,128)} %get-tuple-element.49) | copy-start | bytes 4718596
  228.3 17.4 %all-to-all-start.4 = ((bf16[8,10,1536]{2,1,0:T(8,128)(2,1)}), bf16[8,10,1536]{2,1,0:T(8,128)(2,1)S(1)}, u32[]{:S(2)}, u32[]{:S(2)}) async-start(bf16[8,10,1536]{2,1,0:T(8,128)(2,1)} %pad_maximum_fusion.4), calls=%async_computation.4 | async-start | bytes 786432 | tf_op jit(solution)/shard_map/all_to_all | solution.py:442
  232.6 1.4 copy-start.6
  233.9 11.8 %copy-start.58 = (pred[8]{0:T(512)(128)(4,1)S(1)}, pred[8]{0:T(512)(128)(4,1)}, u32[]{:S(2)}) copy-start(pred[8]{0:T(512)(128)(4,1)} %constant.86.clone.1) | copy-start | bytes 28
  245.8 53.0 %all-to-all-start.5 = ((bf16[64,72,128]{2,1,0:T(8,128)(2,1)}), bf16[64,72,128]{2,1,0:T(8,128)(2,1)S(1)}, u32[]{:S(2)}, u32[]{:S(2)}) async-start(bf16[64,72,128]{2,1,0:T(8,128)(2,1)} %pad_maximum_fusion.2), calls=%async_computation.5 | async-start | bytes 2359296 | tf_op jit(solution)/shard_map/all_to_all | solution.py:408
  300.1 20.4 %all-to-all-start.6 = ((bf16[8,56,1536]{2,1,0:T(8,128)(2,1)}), bf16[8,56,1536]{2,1,0:T(8,128)(2,1)S(1)}, u32[]{:S(2)}, u32[]{:S(2)}) async-start(bf16[8,56,1536]{2,1,0:T(8,128)(2,1)} %broadcast_in_dim.11), calls=%async_computation.6 | async-start | bytes 2752512 | tf_op jit(solution)/shard_map/all_to_all | solution.py:453
  306.8 2.5 collective-permute-start.13
  309.3 0.8 copy-start.5
  315.0 4.3 %copy-start.10 = (bf16[2,64,1536]{2,1,0:T(8,128)(2,1)S(1)}, bf16[2,64,1536]{2,1,0:T(8,128)(2,1)}, u32[]{:S(2)}) copy-start(bf16[2,64,1536]{2,1,0:T(8,128)(2,1)} %get-tuple-element.56) | copy-start | bytes 1179652
  321.0 2.4 copy-start.14
  (19 other events, 14.6 us)
Sparse Core Ops, SparseCore 0:
  9.8 58.6 all-gather.1
